TPU v7x, 512 devices: a whole 4x8x8 slice. The times are simulated.
512 devices in a mesh: region: 128 (over z, y, core), sub: 4 (over x).
Axes of the slice: x: 4, y: 8, z: 8, core: 2. Of those that a mesh axis runs over, the one named last changes fastest.
Arguments:
- modal_state: float32 [9, 56, 65536], P(None, None, ('region', 'sub')), may hold values from -6 to 6
- deriv_stiff: float32 [3, 56, 56], replicated, may hold values from -0.75 to 0.75
- volume_stiff: float32 [3, 56, 56], replicated, may hold values from -0.5 to 0.5
- local_flux: float32 [4, 56, 56], replicated, may hold values from -0.375 to 0.375
- neighbour_flux: float32 [4, 12, 56, 56], replicated, may hold values from -0.375 to 0.375
- star_matrices: float32 [3, 9, 9, 65536], P(None, None, None, ('region', 'sub')), may hold values from -2 to 2
- plus_flux: float32 [4, 9, 9, 65536], P(None, None, None, ('region', 'sub')), may hold values from -2 to 2
- minus_flux: float32 [4, 9, 9, 65536], P(None, None, None, ('region', 'sub')), may hold values from -2 to 2
- cluster_ids: int32 [65536], P(('region', 'sub')), may hold values from 0 to 2
- face_neighbours: int32 [4, 65536], P(None, ('region', 'sub')), may hold values from 0 to 287
- face_orient: int32 [4, 65536], P(None, ('region', 'sub')), may hold values from 0 to 11
- send_lists: int32 [512, 4, 3, 32], P(('region', 'sub')), may hold values from 0 to 127
- sub_lists: int32 [512, 3, 8], P(('region', 'sub')), may hold values from 0 to 127
Outputs:
- new_state: float32 [9, 56, 65536], P(None, None, ('region', 'sub'))
Inputs may be any that keep to these rules, and one draw needn't show every extreme that they name: `face_neighbours`: values below 128 name elements of the same partition, the next 128 name slots received from neighbouring regions, the last 32 slots received from the region's subpartitions. `send_lists`: every slot of every list is used. `sub_lists`: every slot of every list is used.
All inputs are finite; a program needn't handle non-finite values.
Results may differ from a plain program's by a relative error of at most 0.0003.
Values sent between devices are 32-bit elements; how exact they have to be, the bound alone decides.
A program may use at most 128 MiB of HBM per device.

v0:
```python
import jax
import jax.numpy as jnp
from jax import lax
from jax.sharding import PartitionSpec as P

NDER = 6


base_step = 0.25
offset_table = (-2, -1, 1, 2)


def passed_along(value, axis, steps):
    count = lax.axis_size(axis)
    pairs = [(source, (source + steps) % count) for source in range(count)]
    return lax.ppermute(value, axis, pairs)


def apply_small(matrix, values):
    running = matrix[:, 0, :][None, :, :] * values[:, 0, :][:, None, :]
    for column in range(1, values.shape[1]):
        running = running + matrix[:, column, :][None, :, :] * values[:, column, :][:, None, :]
    return running


def apply_modes(matrix, values):
    mode_in, quant_count, local_count = values.shape
    product = jnp.dot(
        matrix,
        values.reshape(mode_in, quant_count * local_count),
        precision=lax.Precision.HIGHEST,
        preferred_element_type=jnp.float32,
    )
    return product.reshape(matrix.shape[0], quant_count, local_count)


def predict(start_state, stars, deriv_stiff, cluster_count):
    series = [start_state]
    current = start_state
    for deriv_order in range(NDER - 1):
        running = jnp.zeros_like(current)
        for direction in range(3):
            running = running + apply_small(
                stars[direction], apply_modes(deriv_stiff[direction], current)
            )
        current = -running
        series.append(current)
    results = []
    for cluster in range(cluster_count):
        step_width = base_step * 2.0**cluster
        running = jnp.zeros_like(start_state)
        factor = 1.0
        for deriv_order in range(NDER):
            factor = factor * step_width / (deriv_order + 1)
            running = running + factor * series[deriv_order]
        results.append(running)
    return jnp.stack(results)


def local(
    modal_state,
    deriv_stiff,
    volume_stiff,
    local_flux,
    neighbour_flux,
    star_matrices,
    plus_flux,
    minus_flux,
    cluster_ids,
    face_neighbours,
    face_orient,
    send_lists,
    sub_lists,
):
    quant_count, mode_count, local_count = modal_state.shape
    send_table = send_lists[0]
    cluster_count = send_table.shape[1]
    slot_count = send_table.shape[2]
    sub_slots = sub_lists.shape[2]
    orient_count = neighbour_flux.shape[1]
    state_modes = jnp.transpose(modal_state, (1, 0, 2))
    integrals = predict(state_modes, star_matrices, deriv_stiff, cluster_count)

    def pack(rows):
        picked = jnp.stack(
            [
                jnp.take(integrals[cluster], rows[cluster], axis=2)
                for cluster in range(cluster_count)
            ]
        )
        return picked.reshape(-1)

    outgoing = [pack(send_table[block_index]) for block_index in range(4)]
    arriving = []
    for block_index in range(4):
        arriving.append(
            passed_along(outgoing[3 - block_index], "region", -offset_table[block_index])
        )
    sub_flat = pack(sub_lists[0])
    sub_all = lax.all_gather(sub_flat[None], "sub", axis=0, tiled=True)
    sub_count = sub_all.shape[0]
    own_integral = jnp.zeros_like(state_modes)
    for cluster in range(cluster_count):
        own_integral = jnp.where(
            cluster_ids[None, None, :] == cluster, integrals[cluster], own_integral
        )
    result = state_modes
    for direction in range(3):
        result = result + apply_small(
            star_matrices[direction], apply_modes(volume_stiff[direction], own_integral)
        )
    region_ghost = jnp.stack(arriving).reshape(
        4, cluster_count, mode_count, quant_count, slot_count
    )
    region_ghost = region_ghost.transpose(1, 2, 3, 0, 4).reshape(
        cluster_count, mode_count, quant_count, 4 * slot_count
    )
    sub_ghost = sub_all.reshape(sub_count, cluster_count, mode_count, quant_count, sub_slots)
    sub_ghost = sub_ghost.transpose(1, 2, 3, 0, 4).reshape(
        cluster_count, mode_count, quant_count, sub_count * sub_slots
    )
    partner_pool = jnp.concatenate([integrals, region_ghost, sub_ghost], axis=3)
    pool_width = partner_pool.shape[3]
    pool_flat = partner_pool.transpose(1, 2, 0, 3).reshape(
        mode_count, quant_count, cluster_count * pool_width
    )
    orient_range = jnp.arange(orient_count, dtype=jnp.int32)
    for face_index in range(4):
        result = result - apply_small(
            plus_flux[face_index], apply_modes(local_flux[face_index], own_integral)
        )
        pool_index = cluster_ids * pool_width + face_neighbours[face_index]
        partner = jnp.take(pool_flat, pool_index, axis=2)
        mixed = apply_small(minus_flux[face_index], partner)
        stacked = neighbour_flux[face_index].reshape(orient_count * mode_count, mode_count)
        every_orient = apply_modes(stacked, mixed).reshape(
            orient_count, mode_count, quant_count, local_count
        )
        onehot = (face_orient[face_index][None, :] == orient_range[:, None]).astype(jnp.float32)
        selected = jnp.sum(every_orient * onehot[:, None, None, :], axis=0)
        result = result - selected
    return jnp.transpose(result, (1, 0, 2))


def solution(mesh):
    return jax.shard_map(
        local,
        mesh=mesh,
        in_specs=(
            P(None, None, ("region", "sub")),
            P(),
            P(),
            P(),
            P(),
            P(None, None, None, ("region", "sub")),
            P(None, None, None, ("region", "sub")),
            P(None, None, None, ("region", "sub")),
            P(("region", "sub")),
            P(None, ("region", "sub")),
            P(None, ("region", "sub")),
            P(("region", "sub"), None, None, None),
            P(("region", "sub"), None, None),
        ),
        out_specs=P(None, None, ("region", "sub")),
        check_vma=False,
    )
```

profile of v0, /device:TPU:1, one launch (start us, length us, event | category | flops | bytes accessed | tf_op | source)
XLA Modules:
  0.0 466.6 jit_solution(817705912703230702)
XLA Ops:
  25.9 9.3 %add_negate_fusion.4 = f32[56,9,128]{0,1,2:T(8,128)S(1)} fusion(f32[56,128]{0,1:T(8,128)} %copy.308, f32[9,128]{0,1:T(8,128)S(1)} %bitcast.1155, f32[56,128]{0,1:T(8,128)} %copy.306, f32[9,128]{0,1:T(8,128)S(1)} %bitcast.1150, f32[56,128]{0,1:T(8,128)} %copy.304, f32[9,128]{0,1:T(8,128)S(1)} %bitcast.1145, f32[56,128]{0,1:T(8,128)} %copy.302, ...), kind=kLoop, calls=%fused_computation.74 | loop fusion | flops 3483648 | bytes 1156608 | tf_op jit(solution)/shard_map/neg | solution.py:46
  53.5 8.8 %add_negate_fusion.3 = f32[56,9,128]{0,1,2:T(8,128)S(1)} fusion(f32[56,128]{0,1:T(8,128)} %copy.336, f32[56,128]{0,1:T(8,128)} %copy.335, f32[56,128]{0,1:T(8,128)} %copy.334, f32[56,128]{0,1:T(8,128)} %copy.333, f32[56,128]{0,1:T(8,128)} %copy.332, f32[56,128]{0,1:T(8,128)} %copy.331, f32[56,128]{0,1:T(8,128)} %copy.330, f32[56,128]{0,1:T(8,128)} %copy.329, ...), kind=kLoop, calls=%fused_computation.73 | loop fusion | flops 3483648 | bytes 1156608 | tf_op jit(solution)/shard_map/neg | solution.py:46
  80.5 9.0 %add_negate_fusion.2 = f32[56,9,128]{0,1,2:T(8,128)S(1)} fusion(f32[56,128]{0,1:T(8,128)} %copy.364, f32[56,128]{0,1:T(8,128)} %copy.363, f32[56,128]{0,1:T(8,128)} %copy.362, f32[56,128]{0,1:T(8,128)} %copy.361, f32[56,128]{0,1:T(8,128)} %copy.360, f32[56,128]{0,1:T(8,128)} %copy.359, f32[56,128]{0,1:T(8,128)} %copy.358, f32[56,128]{0,1:T(8,128)} %copy.357, ...), kind=kLoop, calls=%fused_computation.72 | loop fusion | flops 3483648 | bytes 1156608 | tf_op jit(solution)/shard_map/neg | solution.py:46
  109.3 8.8 %add_negate_fusion.1 = f32[56,9,128]{0,1,2:T(8,128)S(1)} fusion(f32[56,128]{0,1:T(8,128)} %copy.392, f32[56,128]{0,1:T(8,128)} %copy.391, f32[56,128]{0,1:T(8,128)} %copy.390, f32[56,128]{0,1:T(8,128)} %copy.389, f32[56,128]{0,1:T(8,128)} %copy.388, f32[56,128]{0,1:T(8,128)} %copy.387, f32[56,128]{0,1:T(8,128)} %copy.386, f32[56,128]{0,1:T(8,128)} %copy.385, ...), kind=kLoop, calls=%fused_computation.71 | loop fusion | flops 3483648 | bytes 1156608 | tf_op jit(solution)/shard_map/neg | solution.py:46
  146.4 27.5 %select_select_fusion = (f32[56,9,128]{0,1,2:T(8,128)}, f32[56,9,128]{0,1,2:T(8,128)S(1)}, f32[56,9,128]{0,1,2:T(8,128)S(1)}, f32[56,9,128]{0,1,2:T(8,128)S(1)}) fusion(pred[128]{0:T(512)(128)(4,1)S(1)} %get-tuple-element.436, pred[128]{0:T(512)(128)(4,1)S(1)} %get-tuple-element.434, pred[128]{0:T(512)(128)(4,1)S(1)} %get-tuple-element.435, ...), kind=kLoop, calls=%fused_computation.69 | loop fusion | flops 19676160 | bytes 5285760 | tf_op jit(solution)/shard_map/jit(_where)/select_n | solution.py:104
  175.3 1.8 select_bitcast_fusion.13
  182.6 2.0 pad_maximum_fusion
  184.6 2.9 copy.428
  187.5 2.3 reshape.9370
  189.7 4.0 collective-permute-start
  201.9 2.9 copy.429
  204.7 2.3 reshape.9371
  207.0 4.0 collective-permute-start.1
  219.1 2.9 copy.430
  222.0 2.3 reshape.9372
  224.3 4.5 collective-permute-start.2
  236.9 2.9 copy.431
  239.8 2.3 reshape.9373
  242.1 8.2 %collective-permute-start.3 = (f32[48384]{0:T(1024)}, f32[48384]{0:T(1024)}, u32[]{:S(2)}, u32[]{:S(2)}) collective-permute-start(f32[48384]{0:T(1024)} %reshape.9373), channel_id=1, source_target_pairs={{0,504},{4,508},{8,0},{12,4},{16,8},{20,12},{24,16},{28,20},{32,24... | collective-permute-start | bytes 580616 | tf_op jit(solution)/shard_map/ppermute | solution.py:16
  250.3 2.5 copy.421
  254.1 1.8 convolution_bitcast_fusion.10
  255.9 1.9 convolution_bitcast_fusion.9
  257.8 1.9 convolution_bitcast_fusion.8
  282.7 2.6 copy.437
  287.0 10.7 %all-gather = f32[4,1,12096]{2,1,0:T(1,128)} all-gather(f32[1,1,12096]{2,1,0:T(1,128)S(1)} %reshape.9552), channel_id=1, replica_groups=mesh['region'=128,'sub'=4] {'sub'}, dimensions={0}, use_global_device_ids=true | all-gather | bytes 241920 | tf_op jit(solution)/shard_map/all_gather | solution.py:100
  297.7 2.1 reduce
  299.8 4.7 reshape.9375
  304.5 3.9 copy.438
  308.4 2.2 copy.440
  321.7 2.4 fusion.119
  379.7 5.7 %copy.490 = f32[56,9,3,288]{0,1,3,2:T(8,128)} copy(f32[56,9,3,288]{3,0,1,2:T(8,128)S(1)} %maximum_bitcast_fusion) | data formatting | bytes 3483648 | tf_op jit(solution)/shard_map/reshape | solution.py:124
  385.4 3.8 gather_fusion.15
  389.2 3.8 gather_fusion.16
  395.9 3.6 convolution_bitcast_fusion.3
  399.5 3.0 reshape_reshape.12
  402.5 3.8 fusion.121
  408.0 3.6 convolution_bitcast_fusion.2
  411.6 3.2 reshape_reshape.13
  414.8 3.8 gather_fusion.17
  418.6 3.8 gather_fusion.18
  425.3 3.6 convolution_bitcast_fusion.1
  428.9 3.0 reshape_reshape.14
  431.9 4.2 fusion.123
  437.9 4.3 convolution_bitcast_fusion
  442.3 5.0 %reshape_reshape.15 = f32[12,56,9,128]{3,2,1,0:T(8,128)} reshape(f32[672,1152]{1,0:T(8,128)} %convolution_bitcast_fusion) | data formatting | bytes 6193152 | tf_op jit(solution)/shard_map/reshape;reshape | solution.py:136
  447.2 3.2 multiply_reduce_fusion.3
  450.5 3.9 multiply_reduce_fusion.2
  457.0 8.5 %bitcast_subtract_fusion = f32[9,56,128]{2,0,1:T(8,128)S(1)} fusion(f32[56,9,128]{2,1,0:T(8,128)S(1)} %multiply_reduce_fusion, f32[56,9,128]{2,1,0:T(8,128)S(1)} %multiply_reduce_fusion.1, f32[56,9,128]{2,1,0:T(8,128)S(1)} %multiply_reduce_fusion.2, f32[56,9,128]{2,1,0:T(8,128)S(1)} %multiply_reduce_fusion.3, f32[9,56,128]{2,1,0:T(8,128)S(1)} %copy-done, ...), kind=kLoop, calls=%fused_computation.79 | loop fusion | flops 8386560 | bytes 3644928 | tf_op jit(solution)/shard_map/sub | solution.py:141
  (888 shorter events, 243.8 us)
Async XLA Ops:
  5.7 103.3 %copy-start.1 = (f32[9,1,128]{0,2,1:T(8,128)}, f32[9,1,128]{0,2,1:T(8,128)S(1)}, u32[]{:S(2)}) copy-start(f32[9,1,128]{0,2,1:T(8,128)S(1)} %copy.604) | copy-start | bytes 13828
  5.8 103.2 %copy-start.2 = (f32[9,1,128]{0,2,1:T(8,128)}, f32[9,1,128]{0,2,1:T(8,128)S(1)}, u32[]{:S(2)}) copy-start(f32[9,1,128]{0,2,1:T(8,128)S(1)} %copy.605) | copy-start | bytes 13828
  5.9 103.1 %copy-start.3 = (f32[9,1,128]{0,2,1:T(8,128)}, f32[9,1,128]{0,2,1:T(8,128)S(1)}, u32[]{:S(2)}) copy-start(f32[9,1,128]{0,2,1:T(8,128)S(1)} %copy.606) | copy-start | bytes 13828
  6.0 103.0 %copy-start.4 = (f32[9,1,128]{0,2,1:T(8,128)}, f32[9,1,128]{0,2,1:T(8,128)S(1)}, u32[]{:S(2)}) copy-start(f32[9,1,128]{0,2,1:T(8,128)S(1)} %copy.607) | copy-start | bytes 13828
  6.2 102.8 %copy-start.5 = (f32[9,1,128]{0,2,1:T(8,128)}, f32[9,1,128]{0,2,1:T(8,128)S(1)}, u32[]{:S(2)}) copy-start(f32[9,1,128]{0,2,1:T(8,128)S(1)} %copy.608) | copy-start | bytes 13828
  6.3 102.7 %copy-start.6 = (f32[9,1,128]{0,2,1:T(8,128)}, f32[9,1,128]{0,2,1:T(8,128)S(1)}, u32[]{:S(2)}) copy-start(f32[9,1,128]{0,2,1:T(8,128)S(1)} %copy.609) | copy-start | bytes 13828
  6.4 102.6 %copy-start.7 = (f32[9,1,128]{0,2,1:T(8,128)}, f32[9,1,128]{0,2,1:T(8,128)S(1)}, u32[]{:S(2)}) copy-start(f32[9,1,128]{0,2,1:T(8,128)S(1)} %copy.610) | copy-start | bytes 13828
  6.6 102.4 %copy-start.8 = (f32[9,1,128]{0,2,1:T(8,128)}, f32[9,1,128]{0,2,1:T(8,128)S(1)}, u32[]{:S(2)}) copy-start(f32[9,1,128]{0,2,1:T(8,128)S(1)} %copy.611) | copy-start | bytes 13828
  6.8 102.3 %copy-start.9 = (f32[9,1,128]{0,2,1:T(8,128)}, f32[9,1,128]{0,2,1:T(8,128)S(1)}, u32[]{:S(2)}) copy-start(f32[9,1,128]{0,2,1:T(8,128)S(1)} %copy.612) | copy-start | bytes 13828
  6.9 102.2 %copy-start.10 = (f32[9,1,128]{0,2,1:T(8,128)}, f32[9,1,128]{0,2,1:T(8,128)S(1)}, u32[]{:S(2)}) copy-start(f32[9,1,128]{0,2,1:T(8,128)S(1)} %copy.613) | copy-start | bytes 13828
  7.0 102.1 %copy-start.11 = (f32[9,1,128]{0,2,1:T(8,128)}, f32[9,1,128]{0,2,1:T(8,128)S(1)}, u32[]{:S(2)}) copy-start(f32[9,1,128]{0,2,1:T(8,128)S(1)} %copy.614) | copy-start | bytes 13828
  7.1 102.0 %copy-start.12 = (f32[9,1,128]{0,2,1:T(8,128)}, f32[9,1,128]{0,2,1:T(8,128)S(1)}, u32[]{:S(2)}) copy-start(f32[9,1,128]{0,2,1:T(8,128)S(1)} %copy.615) | copy-start | bytes 13828
  7.2 101.9 %copy-start.13 = (f32[9,1,128]{0,2,1:T(8,128)}, f32[9,1,128]{0,2,1:T(8,128)S(1)}, u32[]{:S(2)}) copy-start(f32[9,1,128]{0,2,1:T(8,128)S(1)} %copy.616) | copy-start | bytes 13828
  7.3 101.7 %copy-start.14 = (f32[9,1,128]{0,2,1:T(8,128)}, f32[9,1,128]{0,2,1:T(8,128)S(1)}, u32[]{:S(2)}) copy-start(f32[9,1,128]{0,2,1:T(8,128)S(1)} %copy.617) | copy-start | bytes 13828
  7.5 101.6 %copy-start.15 = (f32[9,1,128]{0,2,1:T(8,128)}, f32[9,1,128]{0,2,1:T(8,128)S(1)}, u32[]{:S(2)}) copy-start(f32[9,1,128]{0,2,1:T(8,128)S(1)} %copy.618) | copy-start | bytes 13828
  7.6 101.5 %copy-start.16 = (f32[9,1,128]{0,2,1:T(8,128)}, f32[9,1,128]{0,2,1:T(8,128)S(1)}, u32[]{:S(2)}) copy-start(f32[9,1,128]{0,2,1:T(8,128)S(1)} %copy.619) | copy-start | bytes 13828
  8.4 100.7 %copy-start.17 = (f32[9,1,128]{0,2,1:T(8,128)}, f32[9,1,128]{0,2,1:T(8,128)S(1)}, u32[]{:S(2)}) copy-start(f32[9,1,128]{0,2,1:T(8,128)S(1)} %copy.620) | copy-start | bytes 13828
  8.8 100.3 %copy-start.18 = (f32[9,1,128]{0,2,1:T(8,128)}, f32[9,1,128]{0,2,1:T(8,128)S(1)}, u32[]{:S(2)}) copy-start(f32[9,1,128]{0,2,1:T(8,128)S(1)} %copy.621) | copy-start | bytes 13828
  9.0 100.1 %copy-start.19 = (f32[9,1,128]{0,2,1:T(8,128)}, f32[9,1,128]{0,2,1:T(8,128)S(1)}, u32[]{:S(2)}) copy-start(f32[9,1,128]{0,2,1:T(8,128)S(1)} %copy.622) | copy-start | bytes 13828
  9.1 100.0 %copy-start.20 = (f32[9,1,128]{0,2,1:T(8,128)}, f32[9,1,128]{0,2,1:T(8,128)S(1)}, u32[]{:S(2)}) copy-start(f32[9,1,128]{0,2,1:T(8,128)S(1)} %copy.623) | copy-start | bytes 13828
  9.2 99.9 %copy-start.21 = (f32[9,1,128]{0,2,1:T(8,128)}, f32[9,1,128]{0,2,1:T(8,128)S(1)}, u32[]{:S(2)}) copy-start(f32[9,1,128]{0,2,1:T(8,128)S(1)} %copy.624) | copy-start | bytes 13828
  9.4 99.8 %copy-start.22 = (f32[9,1,128]{0,2,1:T(8,128)}, f32[9,1,128]{0,2,1:T(8,128)S(1)}, u32[]{:S(2)}) copy-start(f32[9,1,128]{0,2,1:T(8,128)S(1)} %copy.625) | copy-start | bytes 13828
  10.2 99.0 %copy-start.23 = (f32[9,1,128]{0,2,1:T(8,128)}, f32[9,1,128]{0,2,1:T(8,128)S(1)}, u32[]{:S(2)}) copy-start(f32[9,1,128]{0,2,1:T(8,128)S(1)} %copy.626) | copy-start | bytes 13828
  11.0 98.2 %copy-start.24 = (f32[9,1,128]{0,2,1:T(8,128)}, f32[9,1,128]{0,2,1:T(8,128)S(1)}, u32[]{:S(2)}) copy-start(f32[9,1,128]{0,2,1:T(8,128)S(1)} %copy.627) | copy-start | bytes 13828
  11.8 97.4 %copy-start.25 = (f32[9,1,128]{0,2,1:T(8,128)}, f32[9,1,128]{0,2,1:T(8,128)S(1)}, u32[]{:S(2)}) copy-start(f32[9,1,128]{0,2,1:T(8,128)S(1)} %copy.628) | copy-start | bytes 13828
  39.2 23.1 %copy-start.44 = (f32[56,128]{0,1:T(8,128)}, f32[56,128]{0,1:T(8,128)S(1)}, u32[]{:S(2)}) copy-start(f32[56,128]{0,1:T(8,128)S(1)} %copy.310) | copy-start | bytes 86020
  39.3 23.0 %copy-start.45 = (f32[56,128]{0,1:T(8,128)}, f32[56,128]{0,1:T(8,128)S(1)}, u32[]{:S(2)}) copy-start(f32[56,128]{0,1:T(8,128)S(1)} %copy.311) | copy-start | bytes 86020
  66.2 23.3 %copy-start.53 = (f32[56,128]{0,1:T(8,128)}, f32[56,128]{0,1:T(8,128)S(1)}, u32[]{:S(2)}) copy-start(f32[56,128]{0,1:T(8,128)S(1)} %copy.338) | copy-start | bytes 86020
  66.3 23.2 %copy-start.54 = (f32[56,128]{0,1:T(8,128)}, f32[56,128]{0,1:T(8,128)S(1)}, u32[]{:S(2)}) copy-start(f32[56,128]{0,1:T(8,128)S(1)} %copy.339) | copy-start | bytes 86020
  123.7 22.0 %copy-start.206 = (s32[4,128]{1,0:T(4,128)S(1)}, s32[4,128]{1,0:T(4,128)}, u32[]{:S(2)}) copy-start(s32[4,128]{1,0:T(4,128)} %param.28) | copy-start | bytes 6148
  123.7 22.0 %copy-start.208 = (s32[128]{0:T(128)S(1)}, s32[128]{0:T(128)}, u32[]{:S(2)}) copy-start(s32[128]{0:T(128)} %param.27) | copy-start | bytes 1540
  189.7 181.1 %collective-permute-start = (f32[48384]{0:T(1024)}, f32[48384]{0:T(1024)}, u32[]{:S(2)}, u32[]{:S(2)}) collective-permute-start(f32[48384]{0:T(1024)} %reshape.9370), channel_id=1, source_target_pairs={{0,8},{4,12},{8,16},{12,20},{16,24},{20,28},{24,32},{28,36},{32,40... | collective-permute-start | bytes 580616 | tf_op jit(solution)/shard_map/ppermute | solution.py:16
  207.0 165.4 %collective-permute-start.1 = (f32[48384]{0:T(1024)}, f32[48384]{0:T(1024)}, u32[]{:S(2)}, u32[]{:S(2)}) collective-permute-start(f32[48384]{0:T(1024)} %reshape.9371), channel_id=1, source_target_pairs={{0,4},{4,8},{8,12},{12,16},{16,20},{20,24},{24,28},{28,32},{32,36}... | collective-permute-start | bytes 580616 | tf_op jit(solution)/shard_map/ppermute | solution.py:16
  224.3 149.7 %collective-permute-start.2 = (f32[48384]{0:T(1024)}, f32[48384]{0:T(1024)}, u32[]{:S(2)}, u32[]{:S(2)}) collective-permute-start(f32[48384]{0:T(1024)} %reshape.9372), channel_id=1, source_target_pairs={{0,508},{4,0},{8,4},{12,8},{16,12},{20,16},{24,20},{28,24},{32,28}... | collective-permute-start | bytes 580616 | tf_op jit(solution)/shard_map/ppermute | solution.py:16
  242.1 133.5 %collective-permute-start.3 = (f32[48384]{0:T(1024)}, f32[48384]{0:T(1024)}, u32[]{:S(2)}, u32[]{:S(2)}) collective-permute-start(f32[48384]{0:T(1024)} %reshape.9373), channel_id=1, source_target_pairs={{0,504},{4,508},{8,0},{12,4},{16,8},{20,12},{24,16},{28,20},{32,24... | collective-permute-start | bytes 580616 | tf_op jit(solution)/shard_map/ppermute | solution.py:16
  250.3 24.1 %copy-start.112 = (f32[9,1,128]{2,1,0:T(1,128)S(1)}, f32[9,1,128]{2,1,0:T(1,128)}, u32[]{:S(2)}) copy-start(f32[9,1,128]{2,1,0:T(1,128)} %copy-done.111) | copy-start | bytes 13828
  250.3 24.7 %copy-start.110 = (f32[9,1,128]{2,1,0:T(1,128)S(1)}, f32[9,1,128]{2,1,0:T(1,128)}, u32[]{:S(2)}) copy-start(f32[9,1,128]{2,1,0:T(1,128)} %copy-done.109) | copy-start | bytes 13828
  252.8 21.0 %copy-start.116 = (f32[9,1,128]{2,1,0:T(1,128)S(1)}, f32[9,1,128]{2,1,0:T(1,128)}, u32[]{:S(2)}) copy-start(f32[9,1,128]{2,1,0:T(1,128)} %copy-done.115) | copy-start | bytes 13828
  252.8 21.0 %copy-start.118 = (f32[9,1,128]{2,1,0:T(1,128)S(1)}, f32[9,1,128]{2,1,0:T(1,128)}, u32[]{:S(2)}) copy-start(f32[9,1,128]{2,1,0:T(1,128)} %copy-done.117) | copy-start | bytes 13828
  252.8 21.6 %copy-start.114 = (f32[9,1,128]{2,1,0:T(1,128)S(1)}, f32[9,1,128]{2,1,0:T(1,128)}, u32[]{:S(2)}) copy-start(f32[9,1,128]{2,1,0:T(1,128)} %copy-done.113) | copy-start | bytes 13828
  252.9 22.8 %copy-start.124 = (f32[9,1,128]{2,1,0:T(1,128)S(1)}, f32[9,1,128]{2,1,0:T(1,128)}, u32[]{:S(2)}) copy-start(f32[9,1,128]{2,1,0:T(1,128)} %copy-done.123) | copy-start | bytes 13828
  252.9 22.8 %copy-start.130 = (f32[9,1,128]{2,1,0:T(1,128)S(1)}, f32[9,1,128]{2,1,0:T(1,128)}, u32[]{:S(2)}) copy-start(f32[9,1,128]{2,1,0:T(1,128)} %copy-done.129) | copy-start | bytes 13828
  252.9 23.9 %copy-start.207 = (s32[1,3,8]{2,0,1:T(1,128)S(1)}, s32[1,3,8]{2,0,1:T(1,128)}, u32[]{:S(2)}) copy-start(s32[1,3,8]{2,0,1:T(1,128)} %param.31) | copy-start | bytes 292
  312.5 29.0 %copy-start.34 = (f32[56,1152]{1,0:T(8,128)S(1)}, f32[56,1152]{1,0:T(8,128)}, u32[]{:S(2)}) copy-start(f32[56,1152]{1,0:T(8,128)} %convolution_bitcast_fusion.10) | copy-start | bytes 774148
  313.5 28.9 %copy-start.33 = (f32[56,1152]{1,0:T(8,128)S(1)}, f32[56,1152]{1,0:T(8,128)}, u32[]{:S(2)}) copy-start(f32[56,1152]{1,0:T(8,128)} %convolution_bitcast_fusion.9) | copy-start | bytes 774148
  318.7 24.6 %copy-start.32 = (f32[56,1152]{1,0:T(8,128)S(1)}, f32[56,1152]{1,0:T(8,128)}, u32[]{:S(2)}) copy-start(f32[56,1152]{1,0:T(8,128)} %convolution_bitcast_fusion.8) | copy-start | bytes 774148
  321.7 22.5 %copy-start.31 = (f32[56,1152]{1,0:T(8,128)S(1)}, f32[56,1152]{1,0:T(8,128)}, u32[]{:S(2)}) copy-start(f32[56,1152]{1,0:T(8,128)} %convolution_bitcast_fusion.7) | copy-start | bytes 774148
  324.1 21.0 %copy-start.30 = (f32[56,1152]{1,0:T(8,128)S(1)}, f32[56,1152]{1,0:T(8,128)}, u32[]{:S(2)}) copy-start(f32[56,1152]{1,0:T(8,128)} %convolution_bitcast_fusion.6) | copy-start | bytes 774148
  (169 other events, 1261.5 us)
where the time goes:
time: 476 us; the launch traced here: 467 us
  local copies, waits for them, and re-layouts  274 us (58%)
  other arithmetic  118 us (25%)
  matrix products  38.8 us (8%)
  starting transfers between devices  20.8 us (4%)
  blocking collectives  10.7 us (2%)
    mul x152, local copies, waits for them, and re-layouts, apply_small(): matrix[:, column, :][None, :, :] * values[:, column, :][:, None, :]  70.7 us
    unnamed x545, local copies, waits for them, and re-layouts  66.1 us
    dot_general x26, matrix products, apply_modes(): jnp.dot(matrix, values.reshape(mode_in, quant_count * local_count), preci...  38.8 us
    neg x4, other arithmetic, predict(): current = -running  36 us
    select_n x1, other arithmetic, local(): jnp.where(cluster_ids[None, None, :] == cluster, integrals[cluster], own_...  27.5 us
    another operation x20, other arithmetic, pack(): jnp.stack([jnp.take(integrals[cluster], rows[cluster], axis=2) for cluste...  21.2 us
    ppermute x4, starting transfers between devices, passed_along(): return lax.ppermute(value, axis, pairs)  20.8 us
    gather x15, local copies, waits for them, and re-layouts, pack(): jnp.take(integrals[cluster], rows[cluster], axis=2)  18 us
  transfers between devices with their start and end apart: 4, of which 0 were waited for; matrix products, arithmetic and copies ran while one was open for 33% of the time, Pallas kernels for 0%

commit v1 on v0

v1 whole, which is shorter than its diff:
```python
import functools

import jax
import jax.numpy as jnp
from jax import lax
from jax.experimental import pallas as pl
from jax.experimental.pallas import tpu as pltpu
from jax.sharding import PartitionSpec as P

MESH = pl.DeviceIdType.MESH
F32, BF16 = jnp.float32, jnp.bfloat16

NDER = 6
NCLUS = 3
BASE_STEP = 0.25
OFFSETS = (-2, -1, 1, 2)
M = 56
NQ = 9
E = 128
SLOT = 32
SSUB = 8
NORI = 12
ROWS = 512
REG = NCLUS * SLOT
SUB = NCLUS * SSUB
NCH = 4
TAYLOR = []
for _c in range(NCLUS):
    _factor, _row = 1.0, []
    for _k in range(NDER):
        _factor = _factor * (BASE_STEP * 2.0**_c) / (_k + 1)
        _row.append(_factor)
    TAYLOR.append(_row)


def pieces(x):
    high = x.astype(BF16).astype(F32)
    return high, x - high


def left_stack(a):
    high, low = pieces(a)
    gap = jnp.zeros((a.shape[0], 8), F32)
    return jnp.concatenate([high, gap, high, gap, low, gap, low, gap], axis=1).astype(BF16)


def right_slots(high, low):
    gap = jnp.zeros((8, high.shape[1]), F32)
    half = jnp.concatenate([high, gap, low, gap], axis=0).astype(BF16)
    return jnp.concatenate([half, half], axis=0)


def right_stack(x):
    return right_slots(*pieces(x))


def mm(a, b):
    return jnp.dot(a, b, preferred_element_type=F32)


def body(
    n_region, n_sub,
    state_h, dstiff_h, vstiff_h, lflux_h, nflux_h, star_h, plus_h, minus_h,
    clus_h, nbr_h, orient_h, slist_h, blist_h,
    out_h,
    state, dstiff, vstiff, lflux, nflux, star, plus, minus, clus, nbr, orient, slist, blist,
    dstack, wstack, nstack, xs, ys, integ, ihl, tmp, esel, ohl, ohg, own_y, part, sel, res,
    sbuf, sbsub, gbuf,
    in_sem, out_sem, send_sem, recv_sem, ssend_sem, srecv_sem,
):
    r = lax.axis_index("region")
    s = lax.axis_index("sub")
    regions = [lax.rem(r + (o + n_region), n_region) for o in OFFSETS]
    subs = [lax.rem(s + d, n_sub) for d in range(n_sub)]

    barrier = pltpu.get_barrier_semaphore()
    for j in regions:
        pl.semaphore_signal(barrier, inc=1, device_id=(j, s), device_id_type=MESH)
    for d in range(1, n_sub):
        pl.semaphore_signal(barrier, inc=1, device_id=(r, subs[d]), device_id_type=MESH)

    loads = {}
    for i, (name, src, dst) in enumerate((
        ("dstiff", dstiff_h, dstiff), ("state", state_h, state), ("star", star_h, star),
        ("slist", slist_h, slist), ("blist", blist_h, blist), ("clus", clus_h, clus),
        ("nbr", nbr_h, nbr), ("orient", orient_h, orient), ("vstiff", vstiff_h, vstiff),
        ("lflux", lflux_h, lflux), ("plus", plus_h, plus), ("nflux", nflux_h, nflux),
        ("minus", minus_h, minus),
    )):
        loads[name] = pltpu.make_async_copy(src, dst, in_sem.at[i])
        loads[name].start()

    groups = ((0, 1), (2, 3), (4, 5), (6, 7), (8,))

    integ[:, NQ * M :, :] = jnp.zeros((NCLUS, ROWS - NQ * M, E), F32)
    gbuf[:, 4 * REG + n_sub * SUB :, :] = jnp.zeros((NCH, 512 - 4 * REG - n_sub * SUB, E), F32)

    loads["dstiff"].wait()
    dstack[...] = left_stack(-dstiff[...].reshape(3 * M, M))

    loads["state"].wait()

    def modes(source, target):
        for group in groups:
            y = mm(dstack[...], jnp.concatenate([right_stack(source[q]) for q in group], axis=1))
            for i, q in enumerate(group):
                target[q] = y[:, E * i : E * (i + 1)]

    modes(state, ys)
    for q in range(NQ):
        x = state[q]
        for c in range(NCLUS):
            integ[c, M * q : M * (q + 1), :] = TAYLOR[c][0] * x

    def apply_star(ps):
        acc = [None] * len(ps)
        for q in range(NQ):
            for d in range(3):
                y = ys[q, M * d : M * (d + 1), :]
                for i, p in enumerate(ps):
                    term = star[d, p, q : q + 1, :] * y
                    acc[i] = term if acc[i] is None else acc[i] + term
        return acc

    loads["star"].wait()
    for k in range(1, NDER - 1):
        for ps in ((0, 1, 2), (3, 4, 5), (6, 7, 8)):
            for p, x in zip(ps, apply_star(ps)):
                xs[p] = x
                for c in range(NCLUS):
                    integ[c, M * p : M * (p + 1), :] += TAYLOR[c][k] * x
        modes(xs, ys)

    loads["slist"].wait()
    loads["blist"].wait()
    tmp[...] = jnp.zeros((E, E), F32)
    for o in range(4):
        tmp[8 * o : 8 * o + NCLUS, 0:SLOT] = slist[0, o].astype(F32)
    tmp[32 : 32 + NCLUS, 0:SSUB] = blist[0].astype(F32)
    lists = tmp[...].T
    lane = lax.broadcasted_iota(jnp.int32, (SLOT, E), 1).astype(F32)
    for c in range(NCLUS):
        rows = [
            jnp.where(lists[0:SLOT, 8 * o + c : 8 * o + c + 1] == lane, 1.0, 0.0) for o in range(4)
        ]
        rows.append(jnp.where(lists[0:SSUB, 32 + c : 33 + c] == lane[0:SSUB], 1.0, 0.0))
        rows.append(jnp.zeros((8, E), F32))
        onehot = jnp.concatenate(rows, axis=0).astype(BF16)
        esel[c] = jnp.concatenate([onehot, onehot], axis=1)

    pl.semaphore_wait(barrier, 4 + n_sub - 1)

    sends = []

    def send_chunk(i):
        span = slice(E * i, E * (i + 1))
        for c in range(NCLUS):
            high, low = pieces(integ[c, span, :])
            ihl[c, span, :] = jnp.concatenate([high, low], axis=1).astype(BF16)
            picked = lax.dot_general(
                esel[c], ihl[c, span, :], (((1,), (1,)), ((), ())), preferred_element_type=F32
            )
            for o in range(4):
                sbuf[i, o, SLOT * c : SLOT * (c + 1), :] = picked[SLOT * o : SLOT * (o + 1)]
            sbsub[i, SSUB * c : SSUB * (c + 1), :] = picked[4 * SLOT : 4 * SLOT + SSUB]
        for o in (0, 3, 1, 2):
            b = 3 - o
            copy = pltpu.make_async_remote_copy(
                src_ref=sbuf.at[i, o],
                dst_ref=gbuf.at[i, pl.ds(REG * b, REG), :],
                send_sem=send_sem.at[i, o],
                recv_sem=recv_sem.at[i, b],
                device_id=(regions[o], s),
                device_id_type=MESH,
            )
            copy.start()
            sends.append(copy)
        for d in range(1, n_sub):
            copy = pltpu.make_async_remote_copy(
                src_ref=sbsub.at[i],
                dst_ref=gbuf.at[i, pl.ds(4 * REG + SUB * d, SUB), :],
                send_sem=ssend_sem.at[i, d],
                recv_sem=srecv_sem.at[i, d],
                device_id=(r, subs[d]),
                device_id_type=MESH,
            )
            copy.start()
            sends.append(copy)
        gbuf[i, 4 * REG : 4 * REG + SUB, :] = sbsub[i]

    k = NDER - 1
    for i, ps in enumerate(((0, 1, 2), (3, 4), (5, 6), (7, 8))):
        for p, x in zip(ps, apply_star(ps)):
            for c in range(NCLUS):
                integ[c, M * p : M * (p + 1), :] += TAYLOR[c][k] * x
        send_chunk(i)

    for name in ("clus", "nbr", "orient", "vstiff", "lflux", "plus"):
        loads[name].wait()
    wstack[...] = left_stack(
        jnp.concatenate([vstiff[...].reshape(3 * M, M), -lflux[...].reshape(4 * M, M)], axis=0)
    )
    cl = clus[...]
    for group in groups:
        columns = []
        for q in group:
            span = slice(M * q, M * (q + 1))
            own = jnp.where(
                cl == 0, integ[0, span, :], jnp.where(cl == 1, integ[1, span, :], integ[2, span, :])
            )
            columns.append(right_stack(own))
        y = mm(wstack[...], jnp.concatenate(columns, axis=1))
        for i, q in enumerate(group):
            own_y[q] = y[:, E * i : E * (i + 1)]
    for ps in ((0, 1, 2), (3, 4, 5), (6, 7, 8)):
        acc = [state[p] for p in ps]
        for q in range(NQ):
            for j in range(7):
                y = own_y[q, M * j : M * (j + 1), :]
                for i, p in enumerate(ps):
                    weight = star[j, p, q : q + 1, :] if j < 3 else plus[j - 3, p, q : q + 1, :]
                    acc[i] = acc[i] + weight * y
        for i, p in enumerate(ps):
            res[p] = acc[i]

    row_l = lax.broadcasted_iota(jnp.int32, (NCLUS * E, E), 0)
    row_g = lax.broadcasted_iota(jnp.int32, (512, E), 0)
    for f in range(4):
        v = nbr[f : f + 1, :]
        at_region = v - E
        at_sub = v - 2 * E
        k_region = (at_region >> 5) * REG + cl * SLOT + (at_region & 31)
        k_sub = 4 * REG + ((s - (at_sub >> 3)) & 3) * SUB + cl * SSUB + (at_sub & 7)
        k_local = jnp.where(v < E, cl * E + v, -1)
        k_ghost = jnp.where(v < E, -1, jnp.where(v < 2 * E, k_region, k_sub))
        span = slice(E * f, E * (f + 1))
        ohl[:, span] = jnp.where(row_l == k_local, 1.0, 0.0).astype(BF16)
        ohg[:, span] = jnp.where(row_g == k_ghost, 1.0, 0.0).astype(BF16)

    for i in range(NCH):
        span = slice(E * i, E * (i + 1))
        high = jnp.concatenate([ihl[c, span, 0:E] for c in range(NCLUS)], axis=1)
        low = jnp.concatenate([ihl[c, span, E:] for c in range(NCLUS)], axis=1)
        part[i] = mm(jnp.concatenate([high, low], axis=0), ohl[...])

    loads["nflux"].wait()
    for f in range(4):
        for j in range(NORI // 2):
            pair = nflux[f, 2 * j : 2 * j + 2].reshape(2 * M, M)
            nstack[f, 2 * M * j : 2 * M * (j + 1), :] = left_stack(-pair)
    loads["minus"].wait()

    def partner(h, q, f):
        got, row, end = [], M * q, M * (q + 1)
        while row < end:
            i = row // E
            stop = min(end, E * (i + 1))
            lo = row - E * i + E * h
            got.append(part[i, lo : lo + stop - row, E * f : E * (f + 1)])
            row = stop
        return got[0] if len(got) == 1 else jnp.concatenate(got, axis=0)

    todo = (((0, 1),), ((2, 3),), ((4, 5),), ((6, 7), (8,)))
    for i in range(NCH):
        for o in range(4):
            b = 3 - o
            pltpu.make_async_remote_copy(
                src_ref=sbuf.at[i, o], dst_ref=gbuf.at[i, pl.ds(REG * b, REG), :],
                send_sem=send_sem.at[i, o], recv_sem=recv_sem.at[i, b],
                device_id=(regions[o], s), device_id_type=MESH,
            ).wait_recv()
        for d in range(1, n_sub):
            pltpu.make_async_remote_copy(
                src_ref=sbsub.at[i], dst_ref=gbuf.at[i, pl.ds(4 * REG + SUB * d, SUB), :],
                send_sem=ssend_sem.at[i, d], recv_sem=srecv_sem.at[i, d],
                device_id=(r, subs[d]), device_id_type=MESH,
            ).wait_recv()
        high, low = pieces(gbuf[i].T)
        part[i] += mm(jnp.concatenate([high, low], axis=0).astype(BF16), ohg[...])
        for group in todo[i]:
            for f in range(4):
                columns = [right_slots(partner(0, q, f), partner(1, q, f)) for q in group]
                every = mm(nstack[f], jnp.concatenate(columns, axis=1))
                face = orient[f : f + 1, :]
                for j in range(len(group)):
                    span = slice(E * j, E * (j + 1))
                    chosen = every[0:M, span]
                    for o in range(1, NORI):
                        chosen = jnp.where(face == o, every[M * o : M * (o + 1), span], chosen)
                    sel[len(group) * f + j] = chosen
            last = group == (8,)
            for ps in ((0, 1, 2), (3, 4, 5), (6, 7, 8)):
                acc = [res[p] for p in ps]
                for f in range(4):
                    for j, q in enumerate(group):
                        y = sel[len(group) * f + j]
                        for n, p in enumerate(ps):
                            acc[n] = acc[n] + minus[f, p, q : q + 1, :] * y
                for n, p in enumerate(ps):
                    res[p] = acc[n]
                if last:
                    span = pl.ds(ps[0], len(ps))
                    pltpu.make_async_copy(res.at[span], out_h.at[span], out_sem.at[ps[0] // 3]).start()

    for n in range(3):
        span = pl.ds(3 * n, 3)
        pltpu.make_async_copy(res.at[span], out_h.at[span], out_sem.at[n]).wait()
    for copy in sends:
        copy.wait_send()


def local(n_region, n_sub, state, dstiff, vstiff, lflux, nflux, star, plus, minus, clus, nbr, orient, slist, blist):
    clus = clus.reshape(1, E)
    args = (state, dstiff, vstiff, lflux, nflux, star, plus, minus, clus, nbr, orient, slist, blist)
    vm = pltpu.VMEM
    return pl.pallas_call(
        functools.partial(body, n_region, n_sub),
        out_shape=jax.ShapeDtypeStruct((NQ, M, E), F32),
        in_specs=[pl.BlockSpec(memory_space=pl.ANY)] * len(args),
        out_specs=pl.BlockSpec(memory_space=pl.ANY),
        scratch_shapes=[vm(a.shape, a.dtype) for a in args]
        + [
            vm((3 * M, 256), BF16),
            vm((7 * M, 256), BF16),
            vm((4, NORI * M, 256), BF16),
            vm((NQ, M, E), F32),
            vm((NQ, 3 * M, E), F32),
            vm((NCLUS, ROWS, E), F32),
            vm((NCLUS, ROWS, 2 * E), BF16),
            vm((E, E), F32),
            vm((NCLUS, 144, 2 * E), BF16),
            vm((NCLUS * E, 4 * E), BF16),
            vm((512, 4 * E), BF16),
            vm((NQ, 7 * M, E), F32),
            vm((NCH, 2 * E, 4 * E), F32),
            vm((8, M, E), F32),
            vm((NQ, M, E), F32),
            vm((NCH, 4, REG, E), F32),
            vm((NCH, SUB, E), F32),
            vm((NCH, 512, E), F32),
            pltpu.SemaphoreType.DMA((len(args),)),
            pltpu.SemaphoreType.DMA((3,)),
            pltpu.SemaphoreType.DMA((NCH, 4)),
            pltpu.SemaphoreType.DMA((NCH, 4)),
            pltpu.SemaphoreType.DMA((NCH, n_sub)),
            pltpu.SemaphoreType.DMA((NCH, n_sub)),
        ],
        compiler_params=pltpu.CompilerParams(
            collective_id=0, has_side_effects=True, vmem_limit_bytes=44 * 2**20
        ),
        cost_estimate=pl.CostEstimate(flops=2_000_000_000, bytes_accessed=4_000_000, transcendentals=0),
        name="ader_step",
    )(*args)


def solution(mesh):
    return jax.shard_map(
        functools.partial(local, mesh.shape["region"], mesh.shape["sub"]),
        mesh=mesh,
        in_specs=(
            P(None, None, ("region", "sub")),
            P(),
            P(),
            P(),
            P(),
            P(None, None, None, ("region", "sub")),
            P(None, None, None, ("region", "sub")),
            P(None, None, None, ("region", "sub")),
            P(("region", "sub")),
            P(None, ("region", "sub")),
            P(None, ("region", "sub")),
            P(("region", "sub"), None, None, None),
            P(("region", "sub"), None, None),
        ),
        out_specs=P(None, None, ("region", "sub")),
        check_vma=False,
    )
```

time: 476 us -> 40 us (0.08); the launches traced: 467 us -> 39.5 us
  local copies, waits for them, and re-layouts: 274 us -> 11.9 us
  other arithmetic: 118 us -> 0 us
  matrix products: 38.8 us -> 0 us
  Pallas kernels: 0 us -> 27.6 us
  starting transfers between devices: 20.8 us -> 0 us
  blocking collectives: 10.7 us -> 0 us
    mul x174 -> x0, local copies, waits for them, and re-layouts: 78.7 us -> none  [the longest x152 70.7 us: apply_small(): matrix[:, column, :][None, :, :] * values[:, column, :][:, None, :]]
    unnamed x545 -> x22, local copies, waits for them, and re-layouts: 66.1 us -> 11.9 us
    dot_general x26 -> x0, matrix products: 38.8 us -> none  [apply_modes(): jnp.dot(matrix, values.reshape(mode_in, quant_count * local_count), preci...]
    another operation x20 -> x0, local copies, waits for them, and re-layouts: 37.5 us -> none  [the longest x4 14.1 us: local(): apply_modes(stacked, mixed)]
    neg x4 -> x0, other arithmetic: 36 us -> none  [predict(): current = -running]
    gather x19 -> x0, local copies, waits for them, and re-layouts: 33.1 us -> none  [the longest x15 18 us: pack(): jnp.take(integrals[cluster], rows[cluster], axis=2)]
    select_n x3 -> x0, other arithmetic: 30.2 us -> none  [the longest x1 27.5 us: local(): jnp.where(cluster_ids[None, None, :] == cluster, integrals[cluster], own_...]
    pallas_call x0 -> x1, Pallas kernels: none -> 27.6 us  [local(): pl.pallas_call(functools.partial(body, n_region, n_sub), out_shape=jax.Sh...]
  transfers between devices with their start and end apart: 4 -> 0, of which waited for: 0 -> 0; matrix products, arithmetic and copies ran while one was open for 33% -> 0% of each run, Pallas kernels for 0% -> 0%
where the time goes in v1:
time: 40 us; the launch traced here: 39.5 us
  Pallas kernels  27.6 us (69%)
  local copies, waits for them, and re-layouts  11.9 us (30%)
    pallas_call x1, Pallas kernels, local(): pl.pallas_call(functools.partial(body, n_region, n_sub), out_shape=jax.Sh...  27.6 us
    unnamed x22, local copies, waits for them, and re-layouts  11.9 us

profile of v1, /device:TPU:1, one launch (start us, length us, event | category | flops | bytes accessed | tf_op | source)
XLA Modules:
  0.0 39.5 jit_solution(15251372599426664237)
XLA Ops:
  0.0 0.7 %copy.18.blist_h = s32[1,3,8]{2,1,0:T(4,128)S(1)} copy(s32[1,3,8]{2,0,1:T(1,128)} %param.25) | data formatting | bytes 192 | tf_op args[12]
  0.7 0.7 %copy.17.slist_h = s32[1,4,3,32]{3,2,1,0:T(4,128)S(1)} copy(s32[1,4,3,32]{3,1,2,0:T(4,128)} %param.24) | data formatting | bytes 3072 | tf_op args[11]
  1.4 0.9 %copy.14.star_h = f32[3,9,9,128]{3,2,1,0:T(8,128)S(1)} copy(f32[3,9,9,128]{3,0,2,1:T(4,128)} %param.18) | data formatting | bytes 248832 | tf_op args[5]
  2.3 0.9 %copy.15.plus_h = f32[4,9,9,128]{3,2,1,0:T(8,128)S(1)} copy(f32[4,9,9,128]{3,0,2,1:T(4,128)} %param.19) | data formatting | bytes 331776 | tf_op args[6]
  3.3 0.9 %copy.16.minus_h = f32[4,9,9,128]{3,2,1,0:T(8,128)S(1)} copy(f32[4,9,9,128]{3,0,2,1:T(4,128)} %param.20) | data formatting | bytes 331776 | tf_op args[7]
  4.2 0.0 copy-start
  4.2 1.3 %copy-done = f32[4,12,56,56]{3,2,1,0:T(8,128)S(1)} copy-done((f32[4,12,56,56]{3,2,1,0:T(8,128)S(1)}, f32[4,12,56,56]{3,2,1,0:T(8,128)}, u32[]{:S(2)}) %copy-start) | copy-done | bytes 602136
  5.6 0.0 copy-start.1
  5.6 0.9 %copy-done.1 = f32[9,56,128]{2,1,0:T(8,128)S(1)} copy-done((f32[9,56,128]{2,1,0:T(8,128)S(1)}, f32[9,56,128]{2,1,0:T(8,128)}, u32[]{:S(2)}) %copy-start.1) | copy-done | bytes 258072
  6.5 0.0 copy-start.2
  6.5 0.9 %copy-done.2 = f32[4,56,56]{2,1,0:T(8,128)S(1)} copy-done((f32[4,56,56]{2,1,0:T(8,128)S(1)}, f32[4,56,56]{2,1,0:T(8,128)}, u32[]{:S(2)}) %copy-start.2) | copy-done | bytes 50200
  7.4 0.0 copy-start.3
  7.4 0.9 %copy-done.3 = f32[3,56,56]{2,1,0:T(8,128)S(1)} copy-done((f32[3,56,56]{2,1,0:T(8,128)S(1)}, f32[3,56,56]{2,1,0:T(8,128)}, u32[]{:S(2)}) %copy-start.3) | copy-done | bytes 37656
  8.3 0.0 copy-start.4
  8.3 0.9 %copy-done.4 = f32[3,56,56]{2,1,0:T(8,128)S(1)} copy-done((f32[3,56,56]{2,1,0:T(8,128)S(1)}, f32[3,56,56]{2,1,0:T(8,128)}, u32[]{:S(2)}) %copy-start.4) | copy-done | bytes 37656
  9.2 0.0 copy-start.5
  9.2 0.7 %copy-done.5 = s32[4,128]{1,0:T(4,128)S(1)} copy-done((s32[4,128]{1,0:T(4,128)S(1)}, s32[4,128]{1,0:T(4,128)}, u32[]{:S(2)}) %copy-start.5) | copy-done | bytes 2072
  9.9 0.0 copy-start.6
  9.9 0.7 %copy-done.6 = s32[4,128]{1,0:T(4,128)S(1)} copy-done((s32[4,128]{1,0:T(4,128)S(1)}, s32[4,128]{1,0:T(4,128)}, u32[]{:S(2)}) %copy-start.6) | copy-done | bytes 2072
  10.6 0.0 copy-start.7
  10.6 0.7 %copy-done.7 = s32[128]{0:T(128)S(1)} copy-done((s32[128]{0:T(128)S(1)}, s32[128]{0:T(128)}, u32[]{:S(2)}) %copy-start.7) | copy-done | bytes 536
  11.2 27.6 %ader_step.1 = f32[9,56,128]{2,1,0:T(8,128)S(1)} custom-call(f32[9,56,128]{2,1,0:T(8,128)S(1)} %copy-done.1, f32[3,56,56]{2,1,0:T(8,128)S(1)} %copy-done.3, f32[3,56,56]{2,1,0:T(8,128)S(1)} %copy-done.4, f32[4,56,56]{2,1,0:T(8,128)S(1)} %copy-done.2, f32[4,12,56,56]{3,2,1,0:T(8,128)S(1)} %copy-done, f32[3,9,9,128]{3,2,1,0:T(8,128)S(1)} %copy.14.star_h, ...), custom_call_target="tpu_custom_call" | custom-call | flops 2000000000 | bytes 4000000 | tf_op jit(solution)/shard_map/ader_step/pallas_call | solution.py:316
  38.8 0.7 %copy.20 = f32[9,56,128]{2,1,0:T(8,128)} copy(f32[9,56,128]{2,1,0:T(8,128)S(1)} %ader_step.1) | data formatting | bytes 516096
Async XLA Ops:
  4.2 1.3 %copy-start = (f32[4,12,56,56]{3,2,1,0:T(8,128)S(1)}, f32[4,12,56,56]{3,2,1,0:T(8,128)}, u32[]{:S(2)}) copy-start(f32[4,12,56,56]{3,2,1,0:T(8,128)} %nflux_h.1) | copy-start | bytes 1806340
  5.6 0.9 %copy-start.1 = (f32[9,56,128]{2,1,0:T(8,128)S(1)}, f32[9,56,128]{2,1,0:T(8,128)}, u32[]{:S(2)}) copy-start(f32[9,56,128]{2,1,0:T(8,128)} %state_h.1) | copy-start | bytes 774148
  6.5 0.9 %copy-start.2 = (f32[4,56,56]{2,1,0:T(8,128)S(1)}, f32[4,56,56]{2,1,0:T(8,128)}, u32[]{:S(2)}) copy-start(f32[4,56,56]{2,1,0:T(8,128)} %lflux_h.1) | copy-start | bytes 150532
  7.4 0.9 %copy-start.3 = (f32[3,56,56]{2,1,0:T(8,128)S(1)}, f32[3,56,56]{2,1,0:T(8,128)}, u32[]{:S(2)}) copy-start(f32[3,56,56]{2,1,0:T(8,128)} %dstiff_h.1) | copy-start | bytes 112900
  8.3 0.9 %copy-start.4 = (f32[3,56,56]{2,1,0:T(8,128)S(1)}, f32[3,56,56]{2,1,0:T(8,128)}, u32[]{:S(2)}) copy-start(f32[3,56,56]{2,1,0:T(8,128)} %vstiff_h.1) | copy-start | bytes 112900
  9.2 0.7 %copy-start.5 = (s32[4,128]{1,0:T(4,128)S(1)}, s32[4,128]{1,0:T(4,128)}, u32[]{:S(2)}) copy-start(s32[4,128]{1,0:T(4,128)} %nbr_h.1) | copy-start | bytes 6148
  9.9 0.7 %copy-start.6 = (s32[4,128]{1,0:T(4,128)S(1)}, s32[4,128]{1,0:T(4,128)}, u32[]{:S(2)}) copy-start(s32[4,128]{1,0:T(4,128)} %orient_h.1) | copy-start | bytes 6148
  10.6 0.7 %copy-start.7 = (s32[128]{0:T(128)S(1)}, s32[128]{0:T(128)}, u32[]{:S(2)}) copy-start(s32[128]{0:T(128)} %param.21) | copy-start | bytes 1540

commit v2 on v1

--- a/solution.py
+++ b/solution.py
@@ -23,6 +23,7 @@
 ROWS = 512
 REG = NCLUS * SLOT
 SUB = NCLUS * SSUB
+FROM = 4 * REG + 3 * SUB
 NCH = 4
 TAYLOR = []
 for _c in range(NCLUS):
@@ -62,11 +63,11 @@
     n_region, n_sub,
     state_h, dstiff_h, vstiff_h, lflux_h, nflux_h, star_h, plus_h, minus_h,
     clus_h, nbr_h, orient_h, slist_h, blist_h,
-    out_h,
+    res,
     state, dstiff, vstiff, lflux, nflux, star, plus, minus, clus, nbr, orient, slist, blist,
-    dstack, wstack, nstack, xs, ys, integ, ihl, tmp, esel, ohl, ohg, own_y, part, sel, res,
+    dstack, wstack, nstack, ys, ys2, integ, ihl, tmp, esel, ohl, ohg, own_y, part, sel,
     sbuf, sbsub, gbuf,
-    in_sem, out_sem, send_sem, recv_sem, ssend_sem, srecv_sem,
+    in_sem, send_sem, recv_sem,
 ):
     r = lax.axis_index("region")
     s = lax.axis_index("sub")
@@ -82,14 +83,17 @@
     loads = {}
     for i, (name, src, dst) in enumerate((
         ("dstiff", dstiff_h, dstiff), ("state", state_h, state), ("star", star_h, star),
-        ("slist", slist_h, slist), ("blist", blist_h, blist), ("clus", clus_h, clus),
-        ("nbr", nbr_h, nbr), ("orient", orient_h, orient), ("vstiff", vstiff_h, vstiff),
+        ("slist", slist_h, slist), ("blist", blist_h, blist),
+        ("vstiff", vstiff_h, vstiff),
+        ("clus", clus_h, clus), ("nbr", nbr_h, nbr), ("orient", orient_h, orient),
         ("lflux", lflux_h, lflux), ("plus", plus_h, plus), ("nflux", nflux_h, nflux),
         ("minus", minus_h, minus),
     )):
         loads[name] = pltpu.make_async_copy(src, dst, in_sem.at[i])
-        loads[name].start()
-
+        if i < 5:
+            loads[name].start()
+
+    late = ("vstiff", "clus", "nbr", "orient", "lflux", "plus", "nflux", "minus")
     groups = ((0, 1), (2, 3), (4, 5), (6, 7), (8,))
 
     integ[:, NQ * M :, :] = jnp.zeros((NCLUS, ROWS - NQ * M, E), F32)
@@ -100,57 +104,72 @@
 
     loads["state"].wait()
 
-    def modes(source, target):
-        for group in groups:
-            y = mm(dstack[...], jnp.concatenate([right_stack(source[q]) for q in group], axis=1))
-            for i, q in enumerate(group):
-                target[q] = y[:, E * i : E * (i + 1)]
-
-    modes(state, ys)
+    pairs = ((0, 1), (2, 3), (4, 5), (6, 7), (8,))
+
+    def modes(group, values, target):
+        y = mm(dstack[...], jnp.concatenate([right_stack(x) for x in values], axis=1))
+        for i, q in enumerate(group):
+            target[q] = y[:, E * i : E * (i + 1)]
+
+    for group in pairs:
+        modes(group, [state[q] for q in group], ys)
     for q in range(NQ):
         x = state[q]
         for c in range(NCLUS):
             integ[c, M * q : M * (q + 1), :] = TAYLOR[c][0] * x
 
-    def apply_star(ps):
+    def apply_star(ps, source):
         acc = [None] * len(ps)
         for q in range(NQ):
             for d in range(3):
-                y = ys[q, M * d : M * (d + 1), :]
+                y = source[q, M * d : M * (d + 1), :]
                 for i, p in enumerate(ps):
-                    term = star[d, p, q : q + 1, :] * y
+                    term = star[p, q, d : d + 1, :] * y
                     acc[i] = term if acc[i] is None else acc[i] + term
         return acc
-
-    loads["star"].wait()
-    for k in range(1, NDER - 1):
-        for ps in ((0, 1, 2), (3, 4, 5), (6, 7, 8)):
-            for p, x in zip(ps, apply_star(ps)):
-                xs[p] = x
-                for c in range(NCLUS):
-                    integ[c, M * p : M * (p + 1), :] += TAYLOR[c][k] * x
-        modes(xs, ys)
 
     loads["slist"].wait()
     loads["blist"].wait()
     tmp[...] = jnp.zeros((E, E), F32)
-    for o in range(4):
-        tmp[8 * o : 8 * o + NCLUS, 0:SLOT] = slist[0, o].astype(F32)
-    tmp[32 : 32 + NCLUS, 0:SSUB] = blist[0].astype(F32)
+    for c in range(NCLUS):
+        tmp[8 * c : 8 * c + 4, 0:SLOT] = slist[c].astype(F32)
+        tmp[8 * c + 4 : 8 * c + 5, 0:SSUB] = blist[c].astype(F32)
     lists = tmp[...].T
     lane = lax.broadcasted_iota(jnp.int32, (SLOT, E), 1).astype(F32)
     for c in range(NCLUS):
         rows = [
-            jnp.where(lists[0:SLOT, 8 * o + c : 8 * o + c + 1] == lane, 1.0, 0.0) for o in range(4)
+            jnp.where(lists[0:SLOT, 8 * c + o : 8 * c + o + 1] == lane, 1.0, 0.0) for o in range(4)
         ]
-        rows.append(jnp.where(lists[0:SSUB, 32 + c : 33 + c] == lane[0:SSUB], 1.0, 0.0))
+        rows.append(jnp.where(lists[0:SSUB, 8 * c + 4 : 8 * c + 5] == lane[0:SSUB], 1.0, 0.0))
         rows.append(jnp.zeros((8, E), F32))
         onehot = jnp.concatenate(rows, axis=0).astype(BF16)
         esel[c] = jnp.concatenate([onehot, onehot], axis=1)
 
+    loads["star"].wait()
+    for name in late:
+        loads[name].start()
+
+    def step(k, source, target):
+        weights = []
+        for c in range(NCLUS):
+            weights.append(TAYLOR[c][k])
+        for group in ((0, 1, 2), (3, 4, 5), (6, 7, 8)):
+            xs = apply_star(group, source)
+            modes(group, xs, target)
+            for p, x in zip(group, xs):
+                for c in range(NCLUS):
+                    integ[c, M * p : M * (p + 1), :] += weights[c] * x
+
+    def two_steps(n, carry):
+        step(2 * n + 1, ys, ys2)
+        step(2 * n + 2, ys2, ys)
+        return carry
+
+    two_steps(0, 0)
+    two_steps(1, 0)
+
     pl.semaphore_wait(barrier, 4 + n_sub - 1)
 
-    sends = []
 
     def send_chunk(i):
         span = slice(E * i, E * (i + 1))
@@ -168,29 +187,27 @@
             copy = pltpu.make_async_remote_copy(
                 src_ref=sbuf.at[i, o],
                 dst_ref=gbuf.at[i, pl.ds(REG * b, REG), :],
-                send_sem=send_sem.at[i, o],
-                recv_sem=recv_sem.at[i, b],
+                send_sem=send_sem.at[0],
+                recv_sem=recv_sem.at[i],
                 device_id=(regions[o], s),
                 device_id_type=MESH,
             )
             copy.start()
-            sends.append(copy)
         for d in range(1, n_sub):
             copy = pltpu.make_async_remote_copy(
                 src_ref=sbsub.at[i],
-                dst_ref=gbuf.at[i, pl.ds(4 * REG + SUB * d, SUB), :],
-                send_sem=ssend_sem.at[i, d],
-                recv_sem=srecv_sem.at[i, d],
+                dst_ref=gbuf.at[i, pl.ds(4 * REG + SUB * (d - 1), SUB), :],
+                send_sem=send_sem.at[1],
+                recv_sem=recv_sem.at[i],
                 device_id=(r, subs[d]),
                 device_id_type=MESH,
             )
             copy.start()
-            sends.append(copy)
-        gbuf[i, 4 * REG : 4 * REG + SUB, :] = sbsub[i]
+        gbuf[i, FROM : FROM + SUB, :] = sbsub[i]
 
     k = NDER - 1
     for i, ps in enumerate(((0, 1, 2), (3, 4), (5, 6), (7, 8))):
-        for p, x in zip(ps, apply_star(ps)):
+        for p, x in zip(ps, apply_star(ps, ys)):
             for c in range(NCLUS):
                 integ[c, M * p : M * (p + 1), :] += TAYLOR[c][k] * x
         send_chunk(i)
@@ -218,7 +235,7 @@
             for j in range(7):
                 y = own_y[q, M * j : M * (j + 1), :]
                 for i, p in enumerate(ps):
-                    weight = star[j, p, q : q + 1, :] if j < 3 else plus[j - 3, p, q : q + 1, :]
+                    weight = star[p, q, j : j + 1, :] if j < 3 else plus[p, q, j - 3 : j - 2, :]
                     acc[i] = acc[i] + weight * y
         for i, p in enumerate(ps):
             res[p] = acc[i]
@@ -230,7 +247,7 @@
         at_region = v - E
         at_sub = v - 2 * E
         k_region = (at_region >> 5) * REG + cl * SLOT + (at_region & 31)
-        k_sub = 4 * REG + ((s - (at_sub >> 3)) & 3) * SUB + cl * SSUB + (at_sub & 7)
+        k_sub = 4 * REG + ((s - (at_sub >> 3) + 3) & 3) * SUB + cl * SSUB + (at_sub & 7)
         k_local = jnp.where(v < E, cl * E + v, -1)
         k_ghost = jnp.where(v < E, -1, jnp.where(v < 2 * E, k_region, k_sub))
         span = slice(E * f, E * (f + 1))
@@ -249,6 +266,17 @@
             pair = nflux[f, 2 * j : 2 * j + 2].reshape(2 * M, M)
             nstack[f, 2 * M * j : 2 * M * (j + 1), :] = left_stack(-pair)
     loads["minus"].wait()
+
+    def whole(ref, sem):
+        return pltpu.make_async_remote_copy(
+            src_ref=ref, dst_ref=ref, send_sem=sem, recv_sem=sem, device_id=(regions[0], s), device_id_type=MESH
+        )
+
+    def arrived(ref, sem):
+        whole(ref, sem).wait_recv()
+
+    def left(ref, sem):
+        whole(ref, sem).wait_send()
 
     def partner(h, q, f):
         got, row, end = [], M * q, M * (q + 1)
@@ -262,19 +290,7 @@
 
     todo = (((0, 1),), ((2, 3),), ((4, 5),), ((6, 7), (8,)))
     for i in range(NCH):
-        for o in range(4):
-            b = 3 - o
-            pltpu.make_async_remote_copy(
-                src_ref=sbuf.at[i, o], dst_ref=gbuf.at[i, pl.ds(REG * b, REG), :],
-                send_sem=send_sem.at[i, o], recv_sem=recv_sem.at[i, b],
-                device_id=(regions[o], s), device_id_type=MESH,
-            ).wait_recv()
-        for d in range(1, n_sub):
-            pltpu.make_async_remote_copy(
-                src_ref=sbsub.at[i], dst_ref=gbuf.at[i, pl.ds(4 * REG + SUB * d, SUB), :],
-                send_sem=ssend_sem.at[i, d], recv_sem=srecv_sem.at[i, d],
-                device_id=(r, subs[d]), device_id_type=MESH,
-            ).wait_recv()
+        arrived(gbuf.at[i, pl.ds(0, FROM), :], recv_sem.at[i])
         high, low = pieces(gbuf[i].T)
         part[i] += mm(jnp.concatenate([high, low], axis=0).astype(BF16), ohg[...])
         for group in todo[i]:
@@ -288,42 +304,38 @@
                     for o in range(1, NORI):
                         chosen = jnp.where(face == o, every[M * o : M * (o + 1), span], chosen)
                     sel[len(group) * f + j] = chosen
-            last = group == (8,)
             for ps in ((0, 1, 2), (3, 4, 5), (6, 7, 8)):
                 acc = [res[p] for p in ps]
                 for f in range(4):
                     for j, q in enumerate(group):
                         y = sel[len(group) * f + j]
                         for n, p in enumerate(ps):
-                            acc[n] = acc[n] + minus[f, p, q : q + 1, :] * y
+                            acc[n] = acc[n] + minus[p, q, f : f + 1, :] * y
                 for n, p in enumerate(ps):
                     res[p] = acc[n]
-                if last:
-                    span = pl.ds(ps[0], len(ps))
-                    pltpu.make_async_copy(res.at[span], out_h.at[span], out_sem.at[ps[0] // 3]).start()
-
-    for n in range(3):
-        span = pl.ds(3 * n, 3)
-        pltpu.make_async_copy(res.at[span], out_h.at[span], out_sem.at[n]).wait()
-    for copy in sends:
-        copy.wait_send()
+
+    left(sbuf, send_sem.at[0])
+    left(gbuf.at[0, pl.ds(0, NCH * (n_sub - 1) * SUB), :], send_sem.at[1])
 
 
 def local(n_region, n_sub, state, dstiff, vstiff, lflux, nflux, star, plus, minus, clus, nbr, orient, slist, blist):
+    star, plus, minus = (jnp.transpose(a, (1, 2, 0, 3)) for a in (star, plus, minus))
+    slist = jnp.transpose(slist, (0, 2, 1, 3)).reshape(NCLUS, 4, SLOT)
+    blist = jnp.transpose(blist, (1, 0, 2))
     clus = clus.reshape(1, E)
     args = (state, dstiff, vstiff, lflux, nflux, star, plus, minus, clus, nbr, orient, slist, blist)
     vm = pltpu.VMEM
     return pl.pallas_call(
         functools.partial(body, n_region, n_sub),
-        out_shape=jax.ShapeDtypeStruct((NQ, M, E), F32),
-        in_specs=[pl.BlockSpec(memory_space=pl.ANY)] * len(args),
-        out_specs=pl.BlockSpec(memory_space=pl.ANY),
+        out_shape=pltpu.VMEM((NQ, M, E), F32),
+        in_specs=[pl.BlockSpec(memory_space=pltpu.HBM)] * len(args),
+        out_specs=pl.BlockSpec(memory_space=pltpu.VMEM),
         scratch_shapes=[vm(a.shape, a.dtype) for a in args]
         + [
             vm((3 * M, 256), BF16),
             vm((7 * M, 256), BF16),
             vm((4, NORI * M, 256), BF16),
-            vm((NQ, M, E), F32),
+            vm((NQ, 3 * M, E), F32),
             vm((NQ, 3 * M, E), F32),
             vm((NCLUS, ROWS, E), F32),
             vm((NCLUS, ROWS, 2 * E), BF16),
@@ -334,19 +346,15 @@
             vm((NQ, 7 * M, E), F32),
             vm((NCH, 2 * E, 4 * E), F32),
             vm((8, M, E), F32),
-            vm((NQ, M, E), F32),
             vm((NCH, 4, REG, E), F32),
             vm((NCH, SUB, E), F32),
             vm((NCH, 512, E), F32),
             pltpu.SemaphoreType.DMA((len(args),)),
-            pltpu.SemaphoreType.DMA((3,)),
-            pltpu.SemaphoreType.DMA((NCH, 4)),
-            pltpu.SemaphoreType.DMA((NCH, 4)),
-            pltpu.SemaphoreType.DMA((NCH, n_sub)),
-            pltpu.SemaphoreType.DMA((NCH, n_sub)),
+            pltpu.SemaphoreType.DMA((2,)),
+            pltpu.SemaphoreType.DMA((NCH,)),
         ],
         compiler_params=pltpu.CompilerParams(
-            collective_id=0, has_side_effects=True, vmem_limit_bytes=44 * 2**20
+            collective_id=0, has_side_effects=True, vmem_limit_bytes=60 * 2**20
         ),
         cost_estimate=pl.CostEstimate(flops=2_000_000_000, bytes_accessed=4_000_000, transcendentals=0),
         name="ader_step",

time: 40 us -> 27 us (0.68); the launches traced: 39.5 us -> 26.9 us
  local copies, waits for them, and re-layouts: 11.9 us -> 0.7 us
  Pallas kernels: 27.6 us -> 26.2 us
    unnamed x22 -> x1, local copies, waits for them, and re-layouts: 11.9 us -> 0.7 us
    pallas_call x1, Pallas kernels: 27.6 us -> 26.2 us  [local(): pl.pallas_call(functools.partial(body, n_region, n_sub), out_shape=pltpu....]
where the time goes in v2:
time: 27 us; the launch traced here: 26.9 us
  Pallas kernels  26.2 us (97%)
  local copies, waits for them, and re-layouts  0.7 us (3%)
    pallas_call x1, Pallas kernels, local(): pl.pallas_call(functools.partial(body, n_region, n_sub), out_shape=pltpu....  26.2 us
    unnamed x1, local copies, waits for them, and re-layouts  0.7 us

profile of v2, /device:TPU:1, one launch (start us, length us, event | category | flops | bytes accessed | tf_op | source)
XLA Modules:
  0.0 26.9 jit_solution(710342720338586079)
XLA Ops:
  0.0 26.2 %ader_step.1 = f32[9,56,128]{2,1,0:T(8,128)S(1)} custom-call(f32[9,56,128]{2,1,0:T(8,128)} %state_h.1, f32[3,56,56]{2,1,0:T(8,128)} %dstiff_h.1, f32[3,56,56]{2,1,0:T(8,128)} %vstiff_h.1, f32[4,56,56]{2,1,0:T(8,128)} %lflux_h.1, f32[4,12,56,56]{3,2,1,0:T(8,128)} %nflux_h.1, f32[9,9,3,128]{3,2,1,0:T(4,128)} %bitcast.8, f32[9,9,4,128]{3,2,1,0:T(4,128)} %bitcast.9, ...), custom_call_target="tpu_custom_call" | custom-call | flops 2000000000 | bytes 4000000 | tf_op jit(solution)/shard_map/ader_step/pallas_call | solution.py:328
  26.2 0.7 %copy.15 = f32[9,56,128]{2,1,0:T(8,128)} copy(f32[9,56,128]{2,1,0:T(8,128)S(1)} %ader_step.1) | data formatting | bytes 516096

commit v3 on v2

--- a/solution.py
+++ b/solution.py
@@ -24,6 +24,7 @@
 REG = NCLUS * SLOT
 SUB = NCLUS * SSUB
 FROM = 4 * REG + 3 * SUB
+RING = 8
 NCH = 4
 TAYLOR = []
 for _c in range(NCLUS):
@@ -73,12 +74,22 @@
     s = lax.axis_index("sub")
     regions = [lax.rem(r + (o + n_region), n_region) for o in OFFSETS]
     subs = [lax.rem(s + d, n_sub) for d in range(n_sub)]
+    last = (r + 1) // n_region
+    via = min(2 * RING, n_region // 2 + 1) - 1
 
     barrier = pltpu.get_barrier_semaphore()
     for j in regions:
         pl.semaphore_signal(barrier, inc=1, device_id=(j, s), device_id_type=MESH)
     for d in range(1, n_sub):
         pl.semaphore_signal(barrier, inc=1, device_id=(r, subs[d]), device_id_type=MESH)
+
+    @pl.when(r == via)
+    def _():
+        pl.semaphore_signal(barrier, inc=1, device_id=(n_region - 1, s), device_id_type=MESH)
+
+    @pl.when(r == 0)
+    def _():
+        pl.semaphore_signal(barrier, inc=1, device_id=(via, s), device_id_type=MESH)
 
     loads = {}
     for i, (name, src, dst) in enumerate((
@@ -97,7 +108,7 @@
     groups = ((0, 1), (2, 3), (4, 5), (6, 7), (8,))
 
     integ[:, NQ * M :, :] = jnp.zeros((NCLUS, ROWS - NQ * M, E), F32)
-    gbuf[:, 4 * REG + n_sub * SUB :, :] = jnp.zeros((NCH, 512 - 4 * REG - n_sub * SUB, E), F32)
+    gbuf[0:NCH, 4 * REG + n_sub * SUB :, :] = jnp.zeros((NCH, 512 - 4 * REG - n_sub * SUB, E), F32)
 
     loads["dstiff"].wait()
     dstack[...] = left_stack(-dstiff[...].reshape(3 * M, M))
@@ -168,7 +179,7 @@
     two_steps(0, 0)
     two_steps(1, 0)
 
-    pl.semaphore_wait(barrier, 4 + n_sub - 1)
+    pl.semaphore_wait(barrier, 4 + n_sub - 1 + jnp.where((r == via) | (r == n_region - 1), 1, 0))
 
 
     def send_chunk(i):
@@ -184,15 +195,15 @@
             sbsub[i, SSUB * c : SSUB * (c + 1), :] = picked[4 * SLOT : 4 * SLOT + SSUB]
         for o in (0, 3, 1, 2):
             b = 3 - o
-            copy = pltpu.make_async_remote_copy(
+            slot, target = (i + NCH * last, regions[o] + via * last) if o == 2 else (i, regions[o])
+            pltpu.make_async_remote_copy(
                 src_ref=sbuf.at[i, o],
-                dst_ref=gbuf.at[i, pl.ds(REG * b, REG), :],
+                dst_ref=gbuf.at[slot, pl.ds(REG * b, REG), :],
                 send_sem=send_sem.at[0],
-                recv_sem=recv_sem.at[i],
-                device_id=(regions[o], s),
+                recv_sem=recv_sem.at[slot],
+                device_id=(target, s),
                 device_id_type=MESH,
-            )
-            copy.start()
+            ).start()
         for d in range(1, n_sub):
             copy = pltpu.make_async_remote_copy(
                 src_ref=sbsub.at[i],
@@ -277,6 +288,21 @@
 
     def left(ref, sem):
         whole(ref, sem).wait_send()
+
+    @pl.when(r == via)
+    def _():
+        span = pl.ds(REG, REG)
+        for i in range(NCH):
+            arrived(gbuf.at[NCH + i, span, :], recv_sem.at[NCH + i])
+            pltpu.make_async_remote_copy(
+                src_ref=gbuf.at[NCH + i, span, :],
+                dst_ref=gbuf.at[i, span, :],
+                send_sem=send_sem.at[2],
+                recv_sem=recv_sem.at[i],
+                device_id=(0, s),
+                device_id_type=MESH,
+            ).start()
+        left(gbuf.at[0, pl.ds(0, NCH * REG), :], send_sem.at[2])
 
     def partner(h, q, f):
         got, row, end = [], M * q, M * (q + 1)
@@ -348,10 +374,10 @@
             vm((8, M, E), F32),
             vm((NCH, 4, REG, E), F32),
             vm((NCH, SUB, E), F32),
-            vm((NCH, 512, E), F32),
+            vm((2 * NCH, 512, E), F32),
             pltpu.SemaphoreType.DMA((len(args),)),
-            pltpu.SemaphoreType.DMA((2,)),
-            pltpu.SemaphoreType.DMA((NCH,)),
+            pltpu.SemaphoreType.DMA((3,)),
+            pltpu.SemaphoreType.DMA((2 * NCH,)),
         ],
         compiler_params=pltpu.CompilerParams(
             collective_id=0, has_side_effects=True, vmem_limit_bytes=60 * 2**20

time: 27 us -> 25.6 us (0.948)
  the two profiles are of different devices: /device:TPU:1 before, /device:TPU:4 now
where the time goes in v3:
time: 25.6 us; the launch traced here: 25.5 us
  Pallas kernels  24.8 us (97%)
  local copies, waits for them, and re-layouts  0.7 us (3%)
    pallas_call x1, Pallas kernels, local(): pl.pallas_call(functools.partial(body, n_region, n_sub), out_shape=pltpu....  24.8 us
    unnamed x1, local copies, waits for them, and re-layouts  0.7 us

profile of v3, /device:TPU:4, one launch (start us, length us, event | category | flops | bytes accessed | tf_op | source)
XLA Modules:
  0.0 25.5 jit_solution(4885067435157215308)
XLA Ops:
  0.0 24.8 %ader_step.1 = f32[9,56,128]{2,1,0:T(8,128)S(1)} custom-call(f32[9,56,128]{2,1,0:T(8,128)} %state_h.1, f32[3,56,56]{2,1,0:T(8,128)} %dstiff_h.1, f32[3,56,56]{2,1,0:T(8,128)} %vstiff_h.1, f32[4,56,56]{2,1,0:T(8,128)} %lflux_h.1, f32[4,12,56,56]{3,2,1,0:T(8,128)} %nflux_h.1, f32[9,9,3,128]{3,2,1,0:T(4,128)} %bitcast.8, f32[9,9,4,128]{3,2,1,0:T(4,128)} %bitcast.9, ...), custom_call_target="tpu_custom_call" | custom-call | flops 2000000000 | bytes 4000000 | tf_op jit(solution)/shard_map/ader_step/pallas_call | solution.py:354
  24.8 0.7 %copy.15 = f32[9,56,128]{2,1,0:T(8,128)} copy(f32[9,56,128]{2,1,0:T(8,128)S(1)} %ader_step.1) | data formatting | bytes 516096

commit v4 on v3

--- a/solution.py
+++ b/solution.py
@@ -193,7 +193,7 @@
             for o in range(4):
                 sbuf[i, o, SLOT * c : SLOT * (c + 1), :] = picked[SLOT * o : SLOT * (o + 1)]
             sbsub[i, SSUB * c : SSUB * (c + 1), :] = picked[4 * SLOT : 4 * SLOT + SSUB]
-        for o in (0, 3, 1, 2):
+        for o in (2, 3, 0, 1):
             b = 3 - o
             slot, target = (i + NCH * last, regions[o] + via * last) if o == 2 else (i, regions[o])
             pltpu.make_async_remote_copy(

time: 25.6 us -> 25.6 us (level)
  no operation moved by 1% of the time
where the time goes in v4:
time: 25.6 us; the launch traced here: 25.4 us
  Pallas kernels  24.7 us (96%)
  local copies, waits for them, and re-layouts  0.7 us (3%)
    pallas_call x1, Pallas kernels, local(): pl.pallas_call(functools.partial(body, n_region, n_sub), out_shape=pltpu....  24.7 us
    unnamed x1, local copies, waits for them, and re-layouts  0.7 us

profile of v4, /device:TPU:4, one launch (start us, length us, event | category | flops | bytes accessed | tf_op | source)
XLA Modules:
  0.0 25.4 jit_solution(14163943364331037481)
XLA Ops:
  0.0 24.7 %ader_step.1 = f32[9,56,128]{2,1,0:T(8,128)S(1)} custom-call(f32[9,56,128]{2,1,0:T(8,128)} %state_h.1, f32[3,56,56]{2,1,0:T(8,128)} %dstiff_h.1, f32[3,56,56]{2,1,0:T(8,128)} %vstiff_h.1, f32[4,56,56]{2,1,0:T(8,128)} %lflux_h.1, f32[4,12,56,56]{3,2,1,0:T(8,128)} %nflux_h.1, f32[9,9,3,128]{3,2,1,0:T(4,128)} %bitcast.8, f32[9,9,4,128]{3,2,1,0:T(4,128)} %bitcast.9, ...), custom_call_target="tpu_custom_call" | custom-call | flops 2000000000 | bytes 4000000 | tf_op jit(solution)/shard_map/ader_step/pallas_call | solution.py:354
  24.7 0.7 %copy.15 = f32[9,56,128]{2,1,0:T(8,128)} copy(f32[9,56,128]{2,1,0:T(8,128)S(1)} %ader_step.1) | data formatting | bytes 516096
